TPU v7x, 32 devices: a whole 2x2x4 slice. The times are simulated.
32 devices in a mesh: img: 4 (over y, x), ch: 8 (over z, core).
Axes of the slice: x: 2, y: 2, z: 4, core: 2. Of those that a mesh axis runs over, the one named last changes fastest.
Arguments:
- images_in: bfloat16 [256, 49, 2048], P('img'), may hold values from -6 to 6
- labels: int32 [256], P(('img', 'ch')), may hold values from 0 to 999
- loss_wt: int32 [256], P(('img', 'ch')), may hold values from 1 to 32
- placement: int32 [4, 64], P('img'), may hold values from 0 to 63, each once within a row
- w_one: float32 [2048, 512], P(None, 'ch'), may hold values from -0.125 to 0.125
- mom_one: float32 [2048, 512], P(None, 'ch'), may hold values from -0.0029296875 to 0.0029296875
- avg_one: float32 [2048, 512], P(None, 'ch'), may hold values from -0.125 to 0.125
- mask_one: int32 [2048, 512], P(None, 'ch'), may hold values 0 or 1
- rank_one: int32 [2048, 512], P(None, 'ch'), may hold values from 0 to 99
- first_norm_params: float32 [2, 512], P(None, 'ch'), may hold values from 0.5 to 1.5
- mom_bn_one: float32 [2, 512], P(None, 'ch'), may hold values from -0.001953125 to 0.001953125
- avg_bn_one: float32 [2, 512], P(None, 'ch'), may hold values from 0.5 to 1.5
- w_two: float32 [2359296], P(('img', 'ch')), may hold values from -0.09375 to 0.09375
- mom_two: float32 [2359296], P(('img', 'ch')), may hold values from -0.01171875 to 0.01171875
- avg_two: float32 [2359296], P(('img', 'ch')), may hold values from -0.09375 to 0.09375
- mask_two: int32 [2359296], P(('img', 'ch')), may hold values 0 or 1
- rank_two: int32 [2359296], P(('img', 'ch')), may hold values from 0 to 99
- second_norm_params: float32 [2, 512], replicated, may hold values from 0.5 to 1.5
- mom_bn_two: float32 [2, 512], replicated, may hold values from -0.01953125 to 0.01953125
- avg_bn_two: float32 [2, 512], replicated, may hold values from 0.5 to 1.5
- w_head: float32 [512000], P(('img', 'ch')), may hold values from -0.75 to 0.75
- mom_head: float32 [512000], P(('img', 'ch')), may hold values from -0.0029296875 to 0.0029296875
- avg_head: float32 [512000], P(('img', 'ch')), may hold values from -0.75 to 0.75
Outputs:
- loss: float32 [], replicated
- new_w_one: float32 [2048, 512], P(None, 'ch')
- new_mom_one: float32 [2048, 512], P(None, 'ch')
- new_avg_one: float32 [2048, 512], P(None, 'ch')
- new_mask_one: int32 [2048, 512], P(None, 'ch')
- copy_w_one: bfloat16 [2048, 512], P(None, 'ch')
- new_bn_one: float32 [2, 512], P(None, 'ch')
- new_mom_bn_one: float32 [2, 512], P(None, 'ch')
- new_avg_bn_one: float32 [2, 512], P(None, 'ch')
- new_w_two: float32 [2359296], P(('img', 'ch'))
- new_mom_two: float32 [2359296], P(('img', 'ch'))
- new_avg_two: float32 [2359296], P(('img', 'ch'))
- new_mask_two: int32 [2359296], P(('img', 'ch'))
- copy_w_two: bfloat16 [2359296], P(('img', 'ch'))
- new_bn_two: float32 [2, 512], replicated
- new_mom_bn_two: float32 [2, 512], replicated
- new_avg_bn_two: float32 [2, 512], replicated
- new_w_head: float32 [512000], P(('img', 'ch'))
- new_mom_head: float32 [512000], P(('img', 'ch'))
- new_avg_head: float32 [512000], P(('img', 'ch'))
- copy_w_head: bfloat16 [512000], P(('img', 'ch'))
Inputs may be any that keep to these rules, and one draw needn't show every extreme that they name: `placement`: each row is a permutation of 0 to 63.
All inputs are finite; a program needn't handle non-finite values. No bound on the sum of `mask_one` or of `mask_two` on one device may be relied on, other than what follows from the above.
Results may differ from a plain program's by a relative error of at most 0.013.
Values may be sent and summed in bfloat16 or wider, within the bound.
A program may use at most 512 MiB of HBM per device.

v0:
```python
import math
import jax
import jax.numpy as jnp
from jax import lax
from jax.sharding import PartitionSpec as P

SIDE = 7
PIX = 49
DROP = 10
GROW = 10
EPS = 1e-05
MOMENTUM = 0.5


def advance(weight, grad, velocity, rate):
    velocity = MOMENTUM * velocity + grad
    return (weight - rate * (grad + MOMENTUM * velocity), velocity)


def dense_update(weight, grad, velocity, average, rate):
    moved, velocity = advance(weight, grad, velocity, rate)
    return (moved, velocity, 0.5 * average + 0.5 * moved)


def sparse_update(weight, grad, velocity, average, mask, rank, rate):
    moved, velocity = advance(weight, grad, velocity, rate)
    kept = (mask == 1) & (rank >= DROP)
    grown = (mask == 0) & (rank < GROW)
    new_mask = jnp.where(kept | grown, 1, 0).astype(jnp.int32)
    weight = jnp.where(kept, moved, 0.0)
    velocity = jnp.where(kept, velocity, 0.0)
    average = 0.5 * average + 0.5 * weight
    return (weight, velocity, average, new_mask, weight.astype(jnp.bfloat16))


def silu_slope(value):
    sigma = jax.nn.sigmoid(value)
    return sigma * (1.0 + value * (1.0 - sigma))


def apply_batch_norm(z, sums, squares, element_count):
    mean = sums / element_count
    inverse_deviation = lax.rsqrt(squares / element_count - mean * mean + EPS)
    return ((z - mean) * inverse_deviation, inverse_deviation)


def batch_norm_backward(
    norm_gain,
    inverse_deviation,
    output_gradient,
    standardized_input,
    bias_gradient_sum,
    gain_gradient_sum,
    element_count,
):
    return (
        norm_gain
        * inverse_deviation
        * (
            output_gradient
            - bias_gradient_sum / element_count
            - standardized_input * gain_gradient_sum / element_count
        )
    )


def contract_rows(left, right):
    return jnp.einsum("pk,pc->kc", left, right, preferred_element_type=jnp.float32)


def shards(
    images_in,
    labels,
    loss_wt,
    placement,
    w_one,
    mom_one,
    avg_one,
    mask_one,
    rank_one,
    first_norm_params,
    mom_bn_one,
    avg_bn_one,
    w_two,
    mom_two,
    avg_two,
    mask_two,
    rank_two,
    second_norm_params,
    mom_bn_two,
    avg_bn_two,
    w_head,
    mom_head,
    avg_head,
):
    n_img = lax.axis_size("img")
    n_ch = lax.axis_size("ch")
    group = images_in.shape[0]
    element_count = labels.shape[0]
    width = second_norm_params.shape[1]
    classes = w_head.shape[0] * n_img * n_ch // width
    images = element_count * n_img * n_ch
    weights = loss_wt.astype(jnp.float32)
    local_total = jnp.sum(weights)
    total = lax.psum(local_total, ("img", "ch"))
    kernel_part = (w_two * mask_two.astype(jnp.float32)).astype(jnp.bfloat16)
    kernel, head = (
        lax.all_gather(kernel_part, ("img", "ch"), axis=0, tiled=True),
        lax.all_gather(w_head.astype(jnp.bfloat16), ("img", "ch"), axis=0, tiled=True),
    )
    kernel = kernel.reshape(9 * width, width)
    head = head.reshape(width, classes)
    rows = images_in.reshape(group * PIX, images_in.shape[2])
    filt_one = (w_one * mask_one.astype(jnp.float32)).astype(jnp.bfloat16)
    first_conv_output = jnp.dot(rows, filt_one, preferred_element_type=jnp.float32)
    first_feature_sum, first_squares_sum = lax.psum(
        (
            jnp.sum(first_conv_output, axis=0),
            jnp.sum(first_conv_output * first_conv_output, axis=0),
        ),
        "img",
    )
    first_element_count = group * PIX * n_img
    first_standardized_input, first_inverse_deviation = apply_batch_norm(
        first_conv_output, first_feature_sum, first_squares_sum, first_element_count
    )
    first_norm_output = first_norm_params[0] * first_standardized_input + first_norm_params[1]
    first_activation_map = jax.nn.silu(first_norm_output).astype(jnp.bfloat16)
    ordered = first_activation_map.reshape(group, PIX, first_activation_map.shape[1])[placement[0]]
    act_in = lax.all_to_all(ordered, "ch", split_axis=0, concat_axis=2, tiled=True)
    padded = jnp.pad(
        act_in.reshape(element_count, SIDE, SIDE, width), ((0, 0), (1, 1), (1, 1), (0, 0))
    )
    patches = jnp.concatenate(
        [
            padded[:, tap // 3 : tap // 3 + SIDE, tap % 3 : tap % 3 + SIDE, :].reshape(
                element_count * PIX, width
            )
            for tap in range(9)
        ],
        axis=1,
    )
    second_conv_output = jnp.dot(patches, kernel, preferred_element_type=jnp.float32)
    s_two = jnp.sum(second_conv_output, axis=0)
    q_two = jnp.sum(second_conv_output * second_conv_output, axis=0)
    second_feature_sum, second_squares_sum = lax.psum((s_two, q_two), ("img", "ch"))
    second_element_count = images * PIX
    second_standardized_input, second_inverse_deviation = apply_batch_norm(
        second_conv_output, second_feature_sum, second_squares_sum, second_element_count
    )
    second_norm_output = second_norm_params[0] * second_standardized_input + second_norm_params[1]
    pooled = jnp.mean(jax.nn.silu(second_norm_output).reshape(element_count, PIX, width), axis=1)
    pooled_low = pooled.astype(jnp.bfloat16)
    logits = jnp.dot(pooled_low, head, preferred_element_type=jnp.float32)
    top = jnp.max(logits, axis=1, keepdims=True)
    expd = jnp.exp(logits - top)
    denom = jnp.sum(expd, axis=1, keepdims=True)
    lse = top[:, 0] + jnp.log(denom[:, 0])
    onehot = labels[:, None] == jnp.arange(classes, dtype=jnp.int32)[None, :]
    picked = jnp.sum(jnp.where(onehot, logits, 0.0), axis=1)
    share = weights / total
    partial_loss_value = jnp.sum(share * (lse - picked))
    d_logits = (share[:, None] * (expd / denom - onehot.astype(jnp.float32))).astype(jnp.bfloat16)
    g_head = contract_rows(pooled_low, d_logits)
    d_pooled = jnp.einsum("ic,kc->ik", d_logits, head, preferred_element_type=jnp.float32)
    d_act = jnp.broadcast_to(d_pooled[:, None, :] / PIX, (element_count, PIX, width)).reshape(
        element_count * PIX, width
    )
    second_output_gradient = d_act * silu_slope(second_norm_output)
    second_shift_bias, second_norm_gain, loss = lax.psum(
        (
            jnp.sum(second_output_gradient, axis=0),
            jnp.sum(second_output_gradient * second_standardized_input, axis=0),
            partial_loss_value,
        ),
        ("img", "ch"),
    )
    second_preact_gradient = batch_norm_backward(
        second_norm_params[0],
        second_inverse_deviation,
        second_output_gradient,
        second_standardized_input,
        second_shift_bias,
        second_norm_gain,
        second_element_count,
    ).astype(jnp.bfloat16)
    g_kernel = contract_rows(patches, second_preact_gradient)
    d_patches = jnp.einsum(
        "pc,kc->pk", second_preact_gradient, kernel, preferred_element_type=jnp.float32
    )
    d_pad = jnp.zeros((element_count, SIDE + 2, SIDE + 2, width), jnp.float32)
    for tap in range(9):
        piece = d_patches[:, tap * width : (tap + 1) * width].reshape(
            element_count, SIDE, SIDE, width
        )
        d_pad = d_pad.at[:, tap // 3 : tap // 3 + SIDE, tap % 3 : tap % 3 + SIDE, :].add(piece)
    d_act_in = d_pad[:, 1:-1, 1:-1, :].astype(jnp.bfloat16).reshape(element_count, PIX, width)
    d_ordered = lax.all_to_all(d_act_in, "ch", split_axis=2, concat_axis=0, tiled=True)
    d_act_one = jnp.zeros_like(d_ordered).at[placement[0]].set(d_ordered)
    d_act_one = d_act_one.reshape(group * PIX, d_ordered.shape[2]).astype(jnp.float32)
    first_output_gradient = d_act_one * silu_slope(first_norm_output)
    first_shift_bias, first_norm_gain = lax.psum(
        (
            jnp.sum(first_output_gradient, axis=0),
            jnp.sum(first_output_gradient * first_standardized_input, axis=0),
        ),
        "img",
    )
    first_preact_gradient = batch_norm_backward(
        first_norm_params[0],
        first_inverse_deviation,
        first_output_gradient,
        first_standardized_input,
        first_shift_bias,
        first_norm_gain,
        first_element_count,
    ).astype(jnp.bfloat16)
    g_filt = lax.psum(
        contract_rows(rows, first_preact_gradient).astype(jnp.bfloat16), "img"
    ).astype(jnp.float32)
    g_one = g_filt * mask_one.astype(jnp.float32)
    flat_two = g_kernel.reshape(-1)
    flat_head = g_head.reshape(-1)
    whole_two, whole_head = lax.psum((flat_two, flat_head), ("img", "ch"))
    slot = lax.axis_index(("img", "ch"))
    part_two = lax.dynamic_slice_in_dim(whole_two, slot * w_two.shape[0], w_two.shape[0])
    part_head = lax.dynamic_slice_in_dim(whole_head, slot * w_head.shape[0], w_head.shape[0])
    g_two = part_two * mask_two.astype(jnp.float32)
    root = math.sqrt(images)
    one = sparse_update(w_one, g_one, mom_one, avg_one, mask_one, rank_one, 1.3 * root)
    bno = dense_update(
        first_norm_params,
        jnp.stack([first_norm_gain, first_shift_bias]),
        mom_bn_one,
        avg_bn_one,
        8.0 * root,
    )
    two = sparse_update(w_two, g_two, mom_two, avg_two, mask_two, rank_two, 0.25 * root)
    bnt = dense_update(
        second_norm_params,
        jnp.stack([second_norm_gain, second_shift_bias]),
        mom_bn_two,
        avg_bn_two,
        root,
    )
    top_head = dense_update(w_head, part_head, mom_head, avg_head, 40.0)
    return (
        loss,
        one[0],
        one[1],
        one[2],
        one[3],
        one[4],
        bno[0],
        bno[1],
        bno[2],
        two[0],
        two[1],
        two[2],
        two[3],
        two[4],
        bnt[0],
        bnt[1],
        bnt[2],
        top_head[0],
        top_head[1],
        top_head[2],
        top_head[0].astype(jnp.bfloat16),
    )


def solution(mesh):
    in_specs = (
        P("img", None, None),
        P(("img", "ch")),
        P(("img", "ch")),
        P("img", None),
        P(None, "ch"),
        P(None, "ch"),
        P(None, "ch"),
        P(None, "ch"),
        P(None, "ch"),
        P(None, "ch"),
        P(None, "ch"),
        P(None, "ch"),
        P(("img", "ch")),
        P(("img", "ch")),
        P(("img", "ch")),
        P(("img", "ch")),
        P(("img", "ch")),
        P(),
        P(),
        P(),
        P(("img", "ch")),
        P(("img", "ch")),
        P(("img", "ch")),
    )
    out_specs = (
        P(),
        P(None, "ch"),
        P(None, "ch"),
        P(None, "ch"),
        P(None, "ch"),
        P(None, "ch"),
        P(None, "ch"),
        P(None, "ch"),
        P(None, "ch"),
        P(("img", "ch")),
        P(("img", "ch")),
        P(("img", "ch")),
        P(("img", "ch")),
        P(("img", "ch")),
        P(),
        P(),
        P(),
        P(("img", "ch")),
        P(("img", "ch")),
        P(("img", "ch")),
        P(("img", "ch")),
    )
    return jax.shard_map(shards, mesh=mesh, in_specs=in_specs, out_specs=out_specs, check_vma=False)
```

profile of v0, /device:TPU:0, one launch (start us, length us, event | category | flops | bytes accessed | tf_op | source)
XLA Modules:
  0.0 710.3 jit_solution(10829418269710759824)
XLA Ops:
  9.0 16.3 %copy.114 = bf16[64,49,2048]{2,1,0:T(8,128)(2,1)} copy(bf16[64,49,2048]{2,0,1:T(8,128)(2,1)} %param.41) | data formatting | bytes 25690112 | tf_op args[0]
  25.3 13.4 %reshape.534 = bf16[3136,2048]{1,0:T(8,128)(2,1)} reshape(bf16[64,49,2048]{2,1,0:T(8,128)(2,1)} %copy.114) | data formatting | bytes 25690112 | tf_op jit(solution)/shard_map/reshape | solution.py:113
  38.7 8.9 %fusion.28 = (f32[64]{0:T(128)S(1)}, f32[64]{0:T(128)S(1)}, f32[64,3136]{1,0:T(8,128)S(1)}) fusion(bf16[3136,2048]{1,0:T(8,128)(2,1)} %reshape.534, f32[2048,64]{0,1:T(8,128)S(1)} %copy-done.7, s32[2048,64]{0,1:T(8,128)S(1)} %copy-done), kind=kOutput, calls=%fused_computation.120 | convolution fusion | flops 823078784 | bytes 14696960 | tf_op jit(solution)/shard_map/dot_general | solution.py:115
  47.6 11.2 %all-reduce.6 = (f32[64]{0:T(128)S(1)}, f32[64]{0:T(128)S(1)}) all-reduce(f32[64]{0:T(128)S(1)} %get-tuple-element.132, f32[64]{0:T(128)S(1)} %get-tuple-element.131), channel_id=1, replica_groups=mesh['img'=4,'ch'=8] {'img'}, use_global_device_ids=true, to_apply=%region_5.0 | all-reduce | flops 128 | bytes 1024 | tf_op jit(solution)/shard_map/psum | solution.py:116
  65.7 4.9 all-to-all-start
  70.7 56.5 %all-gather = bf16[32,1,16000]{2,1,0:T(2,128)(2,1)S(1)} all-gather(bf16[1,1,16000]{2,1,0:T(2,128)(2,1)S(1)} %reshape.582), channel_id=1, replica_groups=mesh['img'=4,'ch'=8] {'img','ch'}, dimensions={0}, use_global_device_ids=true | all-gather | bytes 1056000 | tf_op jit(solution)/shard_map/all_gather | solution.py:109
  127.3 7.2 %reduce.25 = bf16[32,16000]{1,0:T(8,128)(2,1)} reduce(bf16[32,1,16000]{2,1,0:T(2,128)(2,1)S(1)} %all-gather, bf16[]{:T(256)} %constant.355), dimensions={1}, to_apply=%all-gather.reduce_sub_computation | reduce | bytes 2048002 | tf_op jit(solution)/shard_map/all_gather | solution.py:109
  176.8 8.5 %reshape.546 = bf16[4608,512]{1,0:T(8,128)(2,1)} reshape(bf16[2359296]{0:T(1024)(128)(2,1)} %all-gather.3.cloned.1.call-done) | data formatting | bytes 9437184 | tf_op jit(solution)/shard_map/reshape | solution.py:111
  185.4 5.5 fusion.30
  190.9 37.4 %all-reduce.3 = (f32[]{:T(128)}, f32[512]{0:T(512)S(1)}, f32[512]{0:T(512)S(1)}) all-reduce(f32[]{:T(128)} %convert_reduce_fusion, f32[512]{0:T(512)S(1)} %get-tuple-element.136, f32[512]{0:T(512)S(1)} %get-tuple-element.135), channel_id=1, replica_groups=mesh['img'=4,'ch'=8] {'img','ch'}, use_global_device_ids=true, to_apply=%region_1.0 | all-reduce | flops 1025 | bytes 8200 | tf_op jit(solution)/shard_map/psum | solution.py:105
  235.8 42.0 %all-reduce.2 = (f32[]{:T(128)}, f32[512]{0:T(512)S(1)}, f32[512]{0:T(512)S(1)}) all-reduce(f32[]{:T(128)} %get-tuple-element.166, f32[512]{0:T(512)S(1)} %get-tuple-element.134, f32[512]{0:T(512)S(1)} %get-tuple-element.133), channel_id=1, replica_groups=mesh['img'=4,'ch'=8] {'img','ch'}, use_global_device_ids=true, to_apply=%region_15.16 | all-reduce | flops 1025 | bytes 8200 | tf_op jit(solution)/shard_map/psum | solution.py:170
  278.8 4.4 fusion.39
  297.1 5.4 scatter-add.31
  302.5 4.4 add_select_fusion
  306.9 5.4 scatter-add.34
  319.1 4.1 scatter-add.35
  336.4 4.1 scatter-add.39
  360.2 4.3 scatter-add.44
  372.3 7.4 %convolution_bitcast_fusion = f32[576,4,8,128]{3,2,1,0:T(8,128)} fusion(bf16[392,4608]{1,0:T(8,128)(2,1)} %constant_dynamic-update-slice_fusion, bf16[392,512]{1,0:T(8,128)(2,1)S(1)} %copy-done.4), kind=kOutput, calls=%fused_computation.2 | convolution fusion | flops 1849688064 | bytes 13451264 | tf_op jit(solution)/shard_map/pk,pc->kc/dot_general | solution.py:68
  379.6 9.7 %copy.138 = f32[576,4,8,128]{3,1,2,0:T(4,128)} copy(f32[576,4,8,128]{3,2,1,0:T(8,128)} %convolution_bitcast_fusion) | data formatting | bytes 18874368
  406.9 10.9 %all-reduce.5 = (f32[64]{0:T(128)S(1)}, f32[64]{0:T(128)S(1)}) all-reduce(f32[64]{0:T(128)S(1)} %get-tuple-element.130, f32[64]{0:T(128)S(1)} %get-tuple-element.129), channel_id=1, replica_groups=mesh['img'=4,'ch'=8] {'img'}, use_global_device_ids=true, to_apply=%region_25.26 | all-reduce | flops 128 | bytes 1024 | tf_op jit(solution)/shard_map/psum | solution.py:202
  417.8 7.8 %fusion = bf16[2048,64]{0,1:T(8,128)(2,1)} fusion(bf16[3136,2048]{1,0:T(8,128)(2,1)} %reshape.534, f32[3136,64]{0,1:T(8,128)S(1)} %get-tuple-element.164, f32[64,3136]{1,0:T(8,128)S(1)} %get-tuple-element.201, f32[64]{0:T(128)S(1)} %get-tuple-element.147, f32[64]{0:T(128)S(1)} %broadcast_multiply_fusion.2, f32[64]{0:T(128)S(1)} %get-tuple-element.192, ...), kind=kOutput, calls=%fused_computation.4 | convolution fusion | flops 823820288 | bytes 14714112 | tf_op jit(solution)/shard_map/pk,pc->kc/dot_general | solution.py:68
  433.8 34.6 %all-reduce.10.cloned.1.call-done = bf16[2048,64]{0,1:T(8,128)(2,1)} async-done(((bf16[2048,64]{0,1:T(8,128)(2,1)}), bf16[2048,64]{0,1:T(8,128)(2,1)}) %all-reduce.10.cloned.1.call-update) | async-done | bytes 262160 | tf_op jit(solution)/shard_map/psum | solution.py:218
  472.5 223.9 %all-reduce.12.cloned.1.call-done = (f32[2359296]{0:T(1024)}, f32[512000]{0:T(1024)}) async-done(((f32[2359296]{0:T(1024)}, f32[512000]{0:T(1024)}), (f32[2359296]{0:T(1024)}, f32[512000]{0:T(1024)})) %all-reduce.12.cloned.1.call-update) | async-done | bytes 11485200 | tf_op jit(solution)/shard_map/psum | solution.py:224
  (191 shorter events, 157.1 us)
Async XLA Ops:
  7.2 169.6 %all-gather.3.cloned.1.call-start = ((), (), s32[]{:S(2)}) async-start(), calls=%async_computation.2 | async-start | bytes 4866048 | tf_op jit(solution)/shard_map/all_gather | solution.py:108
  25.3 13.4 %copy-start = (s32[2048,64]{0,1:T(8,128)S(1)}, s32[2048,64]{0,1:T(8,128)}, u32[]{:S(2)}) copy-start(s32[2048,64]{0,1:T(8,128)} %param.48) | copy-start | bytes 1572868
  25.3 13.4 %copy-start.7 = (f32[2048,64]{0,1:T(8,128)S(1)}, f32[2048,64]{0,1:T(8,128)}, u32[]{:S(2)}) copy-start(f32[2048,64]{0,1:T(8,128)} %param.45) | copy-start | bytes 1572868
  38.7 20.1 %copy-start.21 = (f32[2,64]{1,0:T(2,128)S(1)}, f32[2,64]{1,0:T(2,128)}, u32[]{:S(2)}) copy-start(f32[2,64]{1,0:T(2,128)} %param.50) | copy-start | bytes 1540
  47.5 16.1 %copy-start.34 = (s32[1,64]{1,0:T(1,128)S(1)}, s32[1,64]{1,0:T(1,128)}, u32[]{:S(2)}) copy-start(s32[1,64]{1,0:T(1,128)} %param.44) | copy-start | bytes 772
  59.2 11.4 %copy-start.19 = (f32[16000]{0:T(1024)S(1)}, f32[16000]{0:T(1024)}, u32[]{:S(2)}) copy-start(f32[16000]{0:T(1024)} %param.61) | copy-start | bytes 192004
  63.6 70.8 %copy-start.26 = (s32[64]{0:T(128)}, s32[64]{0:T(128)S(1)}, u32[]{:S(2)}) copy-start(s32[64]{0:T(128)S(1)} %fusion.22) | copy-start | bytes 772
  65.7 74.8 %all-to-all-start = ((bf16[8,2,12544]{2,1,0:T(2,128)(2,1)}), bf16[8,2,12544]{2,1,0:T(2,128)(2,1)S(1)}, u32[]{:S(2)}, u32[]{:S(2)}) async-start(bf16[8,2,12544]{2,1,0:T(2,128)(2,1)} %reshape.586), calls=%async_computation | async-start | bytes 802816 | tf_op jit(solution)/shard_map/all_to_all | solution.py:130
  70.7 67.3 %copy-start.32 = (s32[8]{0:T(128)S(1)}, s32[8]{0:T(128)}, u32[]{:S(2)}) copy-start(s32[8]{0:T(128)} %param.43) | copy-start | bytes 100
  70.7 69.1 %copy-start.33 = (s32[4]{0:T(128)S(1)}, s32[4]{0:T(128)}, u32[]{:S(2)}) copy-start(s32[4]{0:T(128)} %constant.333.clone.1) | copy-start | bytes 52
  70.7 69.8 %copy-start.20 = (f32[2,512]{1,0:T(2,128)S(1)}, f32[2,512]{1,0:T(2,128)}, u32[]{:S(2)}) copy-start(f32[2,512]{1,0:T(2,128)} %param.58) | copy-start | bytes 12292
  153.3 8.0 %copy-start.10 = (bf16[8,7,7,512]{3,0,2,1:T(8,128)(2,1)S(1)}, bf16[8,7,7,512]{3,0,2,1:T(8,128)(2,1)}, u32[]{:S(2)}) copy-start(bf16[8,7,7,512]{3,0,2,1:T(8,128)(2,1)} %get-tuple-element.185) | copy-start | bytes 1204228
  161.4 11.1 %copy-start.11 = (bf16[392,512]{1,0:T(8,128)(2,1)S(1)}, bf16[392,512]{1,0:T(8,128)(2,1)}, u32[]{:S(2)}) copy-start(bf16[392,512]{1,0:T(8,128)(2,1)} %reshape.542) | copy-start | bytes 1204228
  162.5 12.7 %copy-start.12 = (bf16[392,512]{1,0:T(8,128)(2,1)S(1)}, bf16[392,512]{1,0:T(8,128)(2,1)}, u32[]{:S(2)}) copy-start(bf16[392,512]{1,0:T(8,128)(2,1)} %reshape.544) | copy-start | bytes 1204228
  163.4 12.6 %copy-start.13 = (bf16[392,512]{1,0:T(8,128)(2,1)S(1)}, bf16[392,512]{1,0:T(8,128)(2,1)}, u32[]{:S(2)}) copy-start(bf16[392,512]{1,0:T(8,128)(2,1)} %reshape.545) | copy-start | bytes 1204228
  190.9 42.4 %copy-start.24 = (s32[8]{0:T(128)S(1)}, s32[8]{0:T(128)}, u32[]{:S(2)}) copy-start(s32[8]{0:T(128)} %param.42) | copy-start | bytes 100
  368.8 20.6 %all-to-all-start.1 = ((bf16[8,2,12544]{2,1,0:T(2,128)(2,1)}), bf16[8,2,12544]{2,1,0:T(2,128)(2,1)S(1)}, u32[]{:S(2)}, u32[]{:S(2)}) async-start(bf16[8,2,12544]{2,1,0:T(2,128)(2,1)} %reshape.588), calls=%async_computation.1 | async-start | bytes 802816 | tf_op jit(solution)/shard_map/all_to_all | solution.py:198
  372.2 96.1 %all-reduce.10.cloned.1.call-start = ((), (), s32[]{:S(2)}) async-start(), calls=%async_computation.3 | async-start | bytes 524288 | tf_op jit(solution)/shard_map/psum | solution.py:218
  417.8 7.9 %copy-start.29 = (f32[8]{0:T(128)S(1)}, f32[8]{0:T(128)}, u32[]{:S(2)}) copy-start(f32[8]{0:T(128)} %copy-done.28) | copy-start | bytes 100
  425.7 270.7 %all-reduce.12.cloned.1.call-start = ((), (), s32[]{:S(2)}) async-start(), calls=%async_computation.4 | async-start | bytes 22970368 | tf_op jit(solution)/shard_map/psum | solution.py:224
  429.6 38.8 %copy-start.8 = (f32[2048,64]{0,1:T(8,128)S(1)}, f32[2048,64]{0,1:T(8,128)}, u32[]{:S(2)}) copy-start(f32[2048,64]{0,1:T(8,128)} %param.45) | copy-start | bytes 1572868
  429.6 38.7 %copy-start.17 = (f32[2048,64]{0,1:T(8,128)S(1)}, f32[2048,64]{0,1:T(8,128)}, u32[]{:S(2)}) copy-start(f32[2048,64]{0,1:T(8,128)} %param.46) | copy-start | bytes 1572868
  430.7 265.6 %copy-start.16 = (f32[73728]{0:T(1024)S(1)}, f32[73728]{0:T(1024)}, u32[]{:S(2)}) copy-start(f32[73728]{0:T(1024)} %param.53) | copy-start | bytes 884740
  470.4 232.9 %copy-start.6 = (f32[2048,64]{0,1:T(8,128)}, f32[2048,64]{0,1:T(8,128)S(1)}, u32[]{:S(2)}) copy-start(f32[2048,64]{0,1:T(8,128)S(1)} %get-tuple-element.163) | copy-start | bytes 1572868
  (16 other events, 57.0 us)
Sparse Core Ops, SparseCore 0:
  11.6 68.7 all-gather.2
  425.8 42.4 all-reduce.9
  475.9 220.4 all-reduce.11
where the time goes:
time: 720 us; the launch traced here: 710 us
  waiting for transfers between devices  259 us (36%)
  local copies, waits for them, and re-layouts  180 us (25%)
  blocking collectives  158 us (22%)
  other arithmetic  54.9 us (8%)
  matrix products  35.2 us (5%)
  between operations  14.8 us (2%)
  starting transfers between devices  8.48 us (1%)
    psum x1, waiting for transfers between devices, shards(): whole_two, whole_head = lax.psum((flat_two, flat_head), ('img', 'ch'))  224 us
    all_gather x1, blocking collectives, shards(): lax.all_gather(w_head.astype(jnp.bfloat16), ('img', 'ch'), axis=0, tiled=...  56.5 us
    unnamed x85, local copies, waits for them, and re-layouts  48.8 us
    psum x1, blocking collectives, shards(): lax.psum((jnp.sum(second_output_gradient, axis=0), jnp.sum(second_output_...  42 us
    psum x1, blocking collectives, shards(): total = lax.psum(local_total, ('img', 'ch'))  37.4 us
    scatter-add x9, local copies, waits for them, and re-layouts, shards(): d_pad.at[:, tap // 3:tap // 3 + SIDE, tap % 3:tap % 3 + SIDE, :].add(piece)  37.3 us
    psum x1, waiting for transfers between devices, shards(): lax.psum(contract_rows(rows, first_preact_gradient).astype(jnp.bfloat16),...  34.6 us
    another operation x11, local copies, waits for them, and re-layouts  18.7 us
  transfers between devices with their start and end apart: 5, of which 2 were waited for; matrix products, arithmetic and copies ran while one was open for 17% of the time, Pallas kernels for 0%

commit v1 on v0

--- a/solution.py
+++ b/solution.py
@@ -168,12 +168,15 @@
     )
     second_output_gradient = d_act * silu_slope(second_norm_output)
     second_shift_bias, second_norm_gain, loss = lax.psum(
-        (
-            jnp.sum(second_output_gradient, axis=0),
-            jnp.sum(second_output_gradient * second_standardized_input, axis=0),
-            partial_loss_value,
+        lax.psum(
+            (
+                jnp.sum(second_output_gradient, axis=0),
+                jnp.sum(second_output_gradient * second_standardized_input, axis=0),
+                partial_loss_value,
+            ),
+            "ch",
         ),
-        ("img", "ch"),
+        "img",
     )
     second_preact_gradient = batch_norm_backward(
         second_norm_params[0],

time: 720 us -> 702 us (0.975)
  blocking collectives: 158 us -> 140 us
    psum x1, blocking collectives: 42 us -> 15.6 us  [shards(): lax.psum((jnp.sum(second_output_gradient, axis=0), jnp.sum(second_output_...]
    psum x1 -> x2, blocking collectives: 10.9 us -> 18.8 us  [shards(): lax.psum(lax.psum((jnp.sum(second_output_gradient, axis=0), jnp.sum(secon...]
  transfers between devices with their start and end apart: 5 -> 5, of which waited for: 2 -> 2; matrix products, arithmetic and copies ran while one was open for 17% -> 18% of each run, Pallas kernels for 0% -> 0%
where the time goes in v1:
time: 702 us; the launch traced here: 692 us
  waiting for transfers between devices  259 us (37%)
  local copies, waits for them, and re-layouts  180 us (26%)
  blocking collectives  140 us (20%)
  other arithmetic  54.9 us (8%)
  matrix products  35.2 us (5%)
  between operations  14.8 us (2%)
  starting transfers between devices  8.69 us (1%)
    psum x1, waiting for transfers between devices, shards(): whole_two, whole_head = lax.psum((flat_two, flat_head), ('img', 'ch'))  224 us
    all_gather x1, blocking collectives, shards(): lax.all_gather(w_head.astype(jnp.bfloat16), ('img', 'ch'), axis=0, tiled=...  56.7 us
    unnamed x85, local copies, waits for them, and re-layouts  48.7 us
    psum x1, blocking collectives, shards(): total = lax.psum(local_total, ('img', 'ch'))  37.3 us
    scatter-add x9, local copies, waits for them, and re-layouts, shards(): d_pad.at[:, tap // 3:tap // 3 + SIDE, tap % 3:tap % 3 + SIDE, :].add(piece)  37.1 us
    psum x1, waiting for transfers between devices, shards(): lax.psum(contract_rows(rows, first_preact_gradient).astype(jnp.bfloat16),...  35.4 us
    psum x2, blocking collectives, shards(): lax.psum(lax.psum((jnp.sum(second_output_gradient, axis=0), jnp.sum(secon...  18.8 us
    another operation x11, local copies, waits for them, and re-layouts  18.7 us
  transfers between devices with their start and end apart: 5, of which 2 were waited for; matrix products, arithmetic and copies ran while one was open for 18% of the time, Pallas kernels for 0%

profile of v1, /device:TPU:0, one launch (start us, length us, event | category | flops | bytes accessed | tf_op | source)
XLA Modules:
  0.0 692.5 jit_solution(16107103533889933318)
XLA Ops:
  9.0 16.2 %copy.114 = bf16[64,49,2048]{2,1,0:T(8,128)(2,1)} copy(bf16[64,49,2048]{2,0,1:T(8,128)(2,1)} %param.41) | data formatting | bytes 25690112 | tf_op args[0]
  25.2 13.4 %reshape.534 = bf16[3136,2048]{1,0:T(8,128)(2,1)} reshape(bf16[64,49,2048]{2,1,0:T(8,128)(2,1)} %copy.114) | data formatting | bytes 25690112 | tf_op jit(solution)/shard_map/reshape | solution.py:113
  38.6 8.8 %fusion.28 = (f32[64]{0:T(128)S(1)}, f32[64]{0:T(128)S(1)}, f32[64,3136]{1,0:T(8,128)S(1)}) fusion(bf16[3136,2048]{1,0:T(8,128)(2,1)} %reshape.534, f32[2048,64]{0,1:T(8,128)S(1)} %copy-done.7, s32[2048,64]{0,1:T(8,128)S(1)} %copy-done), kind=kOutput, calls=%fused_computation.120 | convolution fusion | flops 823078784 | bytes 14696960 | tf_op jit(solution)/shard_map/dot_general | solution.py:115
  47.5 11.2 %all-reduce.7 = (f32[64]{0:T(128)S(1)}, f32[64]{0:T(128)S(1)}) all-reduce(f32[64]{0:T(128)S(1)} %get-tuple-element.132, f32[64]{0:T(128)S(1)} %get-tuple-element.131), channel_id=1, replica_groups=mesh['img'=4,'ch'=8] {'img'}, use_global_device_ids=true, to_apply=%region_5.0 | all-reduce | flops 128 | bytes 1024 | tf_op jit(solution)/shard_map/psum | solution.py:116
  65.6 4.9 all-to-all-start
  70.6 56.7 %all-gather = bf16[32,1,16000]{2,1,0:T(2,128)(2,1)S(1)} all-gather(bf16[1,1,16000]{2,1,0:T(2,128)(2,1)S(1)} %reshape.582), channel_id=1, replica_groups=mesh['img'=4,'ch'=8] {'img','ch'}, dimensions={0}, use_global_device_ids=true | all-gather | bytes 1056000 | tf_op jit(solution)/shard_map/all_gather | solution.py:109
  127.3 7.2 %reduce.25 = bf16[32,16000]{1,0:T(8,128)(2,1)} reduce(bf16[32,1,16000]{2,1,0:T(2,128)(2,1)S(1)} %all-gather, bf16[]{:T(256)} %constant.355), dimensions={1}, to_apply=%all-gather.reduce_sub_computation | reduce | bytes 2048002 | tf_op jit(solution)/shard_map/all_gather | solution.py:109
  176.9 8.5 %reshape.546 = bf16[4608,512]{1,0:T(8,128)(2,1)} reshape(bf16[2359296]{0:T(1024)(128)(2,1)} %all-gather.3.cloned.1.call-done) | data formatting | bytes 9437184 | tf_op jit(solution)/shard_map/reshape | solution.py:111
  185.5 5.5 fusion.30
  191.0 37.3 %all-reduce.2 = (f32[]{:T(128)}, f32[512]{0:T(512)S(1)}, f32[512]{0:T(512)S(1)}) all-reduce(f32[]{:T(128)} %convert_reduce_fusion, f32[512]{0:T(512)S(1)} %get-tuple-element.136, f32[512]{0:T(512)S(1)} %get-tuple-element.135), channel_id=1, replica_groups=mesh['img'=4,'ch'=8] {'img','ch'}, use_global_device_ids=true, to_apply=%region_1.0 | all-reduce | flops 1025 | bytes 8200 | tf_op jit(solution)/shard_map/psum | solution.py:105
  235.8 15.6 %all-reduce.4 = (f32[]{:T(128)}, f32[512]{0:T(512)S(1)}, f32[512]{0:T(512)S(1)}) all-reduce(f32[]{:T(128)} %get-tuple-element.169, f32[512]{0:T(512)S(1)} %get-tuple-element.134, f32[512]{0:T(512)S(1)} %get-tuple-element.133), channel_id=1, replica_groups=mesh['img'=4,'ch'=8] {'ch'}, use_global_device_ids=true, to_apply=%region_15.16 | all-reduce | flops 1025 | bytes 8200 | tf_op jit(solution)/shard_map/psum | solution.py:171
  251.5 9.7 %all-reduce.6 = (f32[512]{0:T(512)S(1)}, f32[512]{0:T(512)S(1)}) all-reduce(f32[512]{0:T(512)S(1)} %get-tuple-element.145, f32[512]{0:T(512)S(1)} %get-tuple-element.146), channel_id=1, replica_groups=mesh['img'=4,'ch'=8] {'img'}, use_global_device_ids=true, to_apply=%region_22.23 | all-reduce | flops 1024 | bytes 8192 | tf_op jit(solution)/shard_map/psum | solution.py:170
  262.2 4.4 fusion.39
  280.4 5.4 scatter-add.31
  285.8 4.4 add_select_fusion
  290.2 5.4 scatter-add.34
  302.3 4.1 scatter-add.35
  334.7 4.1 scatter-add.41
  355.6 7.4 %convolution_bitcast_fusion = f32[576,4,8,128]{3,2,1,0:T(8,128)} fusion(bf16[392,4608]{1,0:T(8,128)(2,1)} %constant_dynamic-update-slice_fusion, bf16[392,512]{1,0:T(8,128)(2,1)S(1)} %copy-done.4), kind=kOutput, calls=%fused_computation.2 | convolution fusion | flops 1849688064 | bytes 13451264 | tf_op jit(solution)/shard_map/pk,pc->kc/dot_general | solution.py:68
  362.9 9.7 %copy.138 = f32[576,4,8,128]{3,1,2,0:T(4,128)} copy(f32[576,4,8,128]{3,2,1,0:T(8,128)} %convolution_bitcast_fusion) | data formatting | bytes 18874368
  390.2 9.1 %all-reduce.5 = (f32[]{:T(128)}, f32[64]{0:T(128)S(1)}, f32[64]{0:T(128)S(1)}) all-reduce(f32[]{:T(128)} %get-tuple-element.144, f32[64]{0:T(128)S(1)} %get-tuple-element.130, f32[64]{0:T(128)S(1)} %get-tuple-element.129), channel_id=1, replica_groups=mesh['img'=4,'ch'=8] {'img'}, use_global_device_ids=true, to_apply=%region_16.17 | all-reduce | flops 129 | bytes 1032 | tf_op jit(solution)/shard_map/psum | solution.py:170
  399.3 7.8 %fusion = bf16[2048,64]{0,1:T(8,128)(2,1)} fusion(bf16[3136,2048]{1,0:T(8,128)(2,1)} %reshape.534, f32[3136,64]{0,1:T(8,128)S(1)} %get-tuple-element.167, f32[64,3136]{1,0:T(8,128)S(1)} %get-tuple-element.204, f32[64]{0:T(128)S(1)} %get-tuple-element.148, f32[64]{0:T(128)S(1)} %broadcast_multiply_fusion.2, f32[64]{0:T(128)S(1)} %get-tuple-element.195, ...), kind=kOutput, calls=%fused_computation.4 | convolution fusion | flops 823820288 | bytes 14714112 | tf_op jit(solution)/shard_map/pk,pc->kc/dot_general | solution.py:68
  415.2 35.4 %all-reduce.11.cloned.1.call-done = bf16[2048,64]{0,1:T(8,128)(2,1)} async-done(((bf16[2048,64]{0,1:T(8,128)(2,1)}), bf16[2048,64]{0,1:T(8,128)(2,1)}) %all-reduce.11.cloned.1.call-update) | async-done | bytes 262160 | tf_op jit(solution)/shard_map/psum | solution.py:221
  454.8 223.8 %all-reduce.13.cloned.1.call-done = (f32[2359296]{0:T(1024)}, f32[512000]{0:T(1024)}) async-done(((f32[2359296]{0:T(1024)}, f32[512000]{0:T(1024)}), (f32[2359296]{0:T(1024)}, f32[512000]{0:T(1024)})) %all-reduce.13.cloned.1.call-update) | async-done | bytes 11485200 | tf_op jit(solution)/shard_map/psum | solution.py:227
  (192 shorter events, 161.4 us)
Async XLA Ops:
  7.2 169.7 %all-gather.3.cloned.1.call-start = ((), (), s32[]{:S(2)}) async-start(), calls=%async_computation.2 | async-start | bytes 4866048 | tf_op jit(solution)/shard_map/all_gather | solution.py:108
  25.2 13.4 %copy-start = (s32[2048,64]{0,1:T(8,128)S(1)}, s32[2048,64]{0,1:T(8,128)}, u32[]{:S(2)}) copy-start(s32[2048,64]{0,1:T(8,128)} %param.48) | copy-start | bytes 1572868
  25.2 13.4 %copy-start.7 = (f32[2048,64]{0,1:T(8,128)S(1)}, f32[2048,64]{0,1:T(8,128)}, u32[]{:S(2)}) copy-start(f32[2048,64]{0,1:T(8,128)} %param.45) | copy-start | bytes 1572868
  38.6 20.1 %copy-start.21 = (f32[2,64]{1,0:T(2,128)S(1)}, f32[2,64]{1,0:T(2,128)}, u32[]{:S(2)}) copy-start(f32[2,64]{1,0:T(2,128)} %param.50) | copy-start | bytes 1540
  47.5 16.1 %copy-start.34 = (s32[1,64]{1,0:T(1,128)S(1)}, s32[1,64]{1,0:T(1,128)}, u32[]{:S(2)}) copy-start(s32[1,64]{1,0:T(1,128)} %param.44) | copy-start | bytes 772
  59.1 11.4 %copy-start.19 = (f32[16000]{0:T(1024)S(1)}, f32[16000]{0:T(1024)}, u32[]{:S(2)}) copy-start(f32[16000]{0:T(1024)} %param.61) | copy-start | bytes 192004
  63.6 71.0 %copy-start.26 = (s32[64]{0:T(128)}, s32[64]{0:T(128)S(1)}, u32[]{:S(2)}) copy-start(s32[64]{0:T(128)S(1)} %fusion.22) | copy-start | bytes 772
  65.6 74.9 %all-to-all-start = ((bf16[8,2,12544]{2,1,0:T(2,128)(2,1)}), bf16[8,2,12544]{2,1,0:T(2,128)(2,1)S(1)}, u32[]{:S(2)}, u32[]{:S(2)}) async-start(bf16[8,2,12544]{2,1,0:T(2,128)(2,1)} %reshape.586), calls=%async_computation | async-start | bytes 802816 | tf_op jit(solution)/shard_map/all_to_all | solution.py:130
  70.6 67.5 %copy-start.32 = (s32[8]{0:T(128)S(1)}, s32[8]{0:T(128)}, u32[]{:S(2)}) copy-start(s32[8]{0:T(128)} %param.43) | copy-start | bytes 100
  70.6 69.2 %copy-start.33 = (s32[4]{0:T(128)S(1)}, s32[4]{0:T(128)}, u32[]{:S(2)}) copy-start(s32[4]{0:T(128)} %constant.333.clone.1) | copy-start | bytes 52
  70.6 69.9 %copy-start.20 = (f32[2,512]{1,0:T(2,128)S(1)}, f32[2,512]{1,0:T(2,128)}, u32[]{:S(2)}) copy-start(f32[2,512]{1,0:T(2,128)} %param.58) | copy-start | bytes 12292
  153.4 8.0 %copy-start.10 = (bf16[8,7,7,512]{3,0,2,1:T(8,128)(2,1)S(1)}, bf16[8,7,7,512]{3,0,2,1:T(8,128)(2,1)}, u32[]{:S(2)}) copy-start(bf16[8,7,7,512]{3,0,2,1:T(8,128)(2,1)} %get-tuple-element.188) | copy-start | bytes 1204228
  161.5 11.1 %copy-start.11 = (bf16[392,512]{1,0:T(8,128)(2,1)S(1)}, bf16[392,512]{1,0:T(8,128)(2,1)}, u32[]{:S(2)}) copy-start(bf16[392,512]{1,0:T(8,128)(2,1)} %reshape.542) | copy-start | bytes 1204228
  162.6 12.7 %copy-start.12 = (bf16[392,512]{1,0:T(8,128)(2,1)S(1)}, bf16[392,512]{1,0:T(8,128)(2,1)}, u32[]{:S(2)}) copy-start(bf16[392,512]{1,0:T(8,128)(2,1)} %reshape.544) | copy-start | bytes 1204228
  163.5 12.6 %copy-start.13 = (bf16[392,512]{1,0:T(8,128)(2,1)S(1)}, bf16[392,512]{1,0:T(8,128)(2,1)}, u32[]{:S(2)}) copy-start(bf16[392,512]{1,0:T(8,128)(2,1)} %reshape.545) | copy-start | bytes 1204228
  191.0 42.3 %copy-start.24 = (s32[8]{0:T(128)S(1)}, s32[8]{0:T(128)}, u32[]{:S(2)}) copy-start(s32[8]{0:T(128)} %param.42) | copy-start | bytes 100
  234.7 16.7 %copy-start.28 = (f32[8]{0:T(128)}, f32[8]{0:T(128)S(1)}, u32[]{:S(2)}) copy-start(f32[8]{0:T(128)S(1)} %get-tuple-element.170) | copy-start | bytes 100
  351.8 20.8 %all-to-all-start.1 = ((bf16[8,2,12544]{2,1,0:T(2,128)(2,1)}), bf16[8,2,12544]{2,1,0:T(2,128)(2,1)S(1)}, u32[]{:S(2)}, u32[]{:S(2)}) async-start(bf16[8,2,12544]{2,1,0:T(2,128)(2,1)} %reshape.588), calls=%async_computation.1 | async-start | bytes 802816 | tf_op jit(solution)/shard_map/all_to_all | solution.py:201
  355.3 95.3 %all-reduce.11.cloned.1.call-start = ((), (), s32[]{:S(2)}) async-start(), calls=%async_computation.3 | async-start | bytes 524288 | tf_op jit(solution)/shard_map/psum | solution.py:221
  407.1 271.4 %all-reduce.13.cloned.1.call-start = ((), (), s32[]{:S(2)}) async-start(), calls=%async_computation.4 | async-start | bytes 22970368 | tf_op jit(solution)/shard_map/psum | solution.py:227
  411.0 39.6 %copy-start.8 = (f32[2048,64]{0,1:T(8,128)S(1)}, f32[2048,64]{0,1:T(8,128)}, u32[]{:S(2)}) copy-start(f32[2048,64]{0,1:T(8,128)} %param.45) | copy-start | bytes 1572868
  411.0 39.6 %copy-start.17 = (f32[2048,64]{0,1:T(8,128)S(1)}, f32[2048,64]{0,1:T(8,128)}, u32[]{:S(2)}) copy-start(f32[2048,64]{0,1:T(8,128)} %param.46) | copy-start | bytes 1572868
  412.2 266.4 %copy-start.16 = (f32[73728]{0:T(1024)S(1)}, f32[73728]{0:T(1024)}, u32[]{:S(2)}) copy-start(f32[73728]{0:T(1024)} %param.53) | copy-start | bytes 884740
  452.7 232.8 %copy-start.6 = (f32[2048,64]{0,1:T(8,128)}, f32[2048,64]{0,1:T(8,128)S(1)}, u32[]{:S(2)}) copy-start(f32[2048,64]{0,1:T(8,128)S(1)} %get-tuple-element.166) | copy-start | bytes 1572868
  (16 other events, 64.0 us)
Sparse Core Ops, SparseCore 0:
  11.6 68.8 all-gather.2
  407.3 43.2 all-reduce.10
  458.1 220.3 all-reduce.12
